TPU v7x, 32 devices: a whole 2x2x4 slice. The times are simulated.
32 devices in a mesh: gx: 16 (over z, x, core), gy: 2 (over y).
Axes of the slice: x: 2, y: 2, z: 4, core: 2. Of those that a mesh axis runs over, the one named last changes fastest.
Arguments:
- potential: float32 [3, 1, 4096, 256], P(None, None, 'gx', 'gy'), may hold values from -8 to 8
- labels: int32 [1, 4096, 256], P(None, 'gx', 'gy'), may hold values from 0 to 7
- principal: float32 [2, 8], replicated, may hold values from 0.5 to 16
- off_diagonal: float32 [3, 8], replicated, may hold values from -0.4 to 0.4
Outputs:
- updated: float32 [3, 1, 4096, 256], P(None, None, 'gx', 'gy')
All inputs are finite; a program needn't handle non-finite values.
Results may differ from a plain program's by a relative error of at most 0.0017.
Values sent between devices are 32-bit elements; how exact they have to be, the bound alone decides.
A program may use at most 64 MiB of HBM per device.

v0:
```python
import jax
import jax.numpy as jnp
from jax import lax
from jax.sharding import PartitionSpec as P


def shifted_2(shard, axis, by):
    size = lax.axis_size(axis)
    return lax.ppermute(shard, axis, [(i, (i + by) % size) for i in range(size)])


def padded_2(cells, sides, width):
    for axis, dim in sides:
        count = lax.axis_size(axis)
        head = lax.slice_in_dim(cells, 0, width, axis=dim)
        tail = lax.slice_in_dim(cells, cells.shape[dim] - width, cells.shape[dim], axis=dim)
        cells = jnp.concatenate(
            [
                lax.ppermute(tail, axis, [(i, (i + 1) % count) for i in range(count)]),
                cells,
                lax.ppermute(head, axis, [((i + 1) % count, i) for i in range(count)]),
            ],
            axis=dim,
        )
    return cells


def harmonic(first, second):
    return 2.0 * first * second / (first + second)


def neighbour(values, offset, axis_dim, filler):
    extent = values.shape[axis_dim]
    dims_pad = list(values.shape)
    dims_pad[axis_dim] = abs(offset)
    padding = jnp.full(tuple(dims_pad), filler, values.dtype)
    if offset > 0:
        retained = lax.slice_in_dim(values, 0, extent - offset, axis=axis_dim)
        return jnp.concatenate([padding, retained], axis_dim)
    retained = lax.slice_in_dim(values, -offset, extent, axis=axis_dim)
    return jnp.concatenate([retained, padding], axis_dim)


def shifted(values, offset, axis_dim, wrap, filler):
    if wrap:
        return jnp.roll(values, offset, axis_dim)
    return neighbour(values, offset, axis_dim, filler)


def cyclic_reduce(sub_diag, main_diag, super_diag, forcing, axis_dim, wrap):
    extent = sub_diag.shape[axis_dim]
    stride = 1
    while stride < extent:
        low_before = shifted(sub_diag, stride, axis_dim, wrap, 0.0)
        main_before = shifted(main_diag, stride, axis_dim, wrap, 1.0)
        high_before = shifted(super_diag, stride, axis_dim, wrap, 0.0)
        rest_before = shifted(forcing, stride, axis_dim + 1, wrap, 0.0)
        low_after = shifted(sub_diag, -stride, axis_dim, wrap, 0.0)
        main_after = shifted(main_diag, -stride, axis_dim, wrap, 1.0)
        high_after = shifted(super_diag, -stride, axis_dim, wrap, 0.0)
        rest_after = shifted(forcing, -stride, axis_dim + 1, wrap, 0.0)
        factor_low = -sub_diag / main_before
        factor_high = -super_diag / main_after
        forcing = forcing + factor_low[None] * rest_before + factor_high[None] * rest_after
        main_diag = main_diag + factor_low * high_before + factor_high * low_after
        sub_diag = factor_low * low_before
        super_diag = factor_high * high_after
        stride = stride * 2
    return forcing / (sub_diag + main_diag + super_diag)[None]


def reduced_rows(tail_row, next_head, low_last, main_last, high_last, force_last):
    reduced_low = -low_last * tail_row[3]
    reduced_main = main_last - low_last * tail_row[4] - high_last * next_head[3]
    reduced_high = -high_last * next_head[4]
    reduced_force = force_last - low_last[None] * tail_row[:3] - high_last[None] * next_head[:3]
    return jnp.concatenate(
        [reduced_low[None], reduced_main[None], reduced_high[None], reduced_force], 0
    )


def spike_solve(sub_diag, main_diag, super_diag, forcing, axis_dim, interface):
    length = sub_diag.shape[axis_dim]
    position = lax.broadcasted_iota(jnp.int32, sub_diag.shape, axis_dim)
    is_last = position == length - 1
    low_inner = jnp.where((position == 0) | is_last, 0.0, sub_diag)
    high_inner = jnp.where((position == length - 2) | is_last, 0.0, super_diag)
    main_inner = jnp.where(is_last, 1.0, main_diag)
    left_spike = jnp.where(position == 0, sub_diag, 0.0)
    right_spike = jnp.where(position == length - 2, super_diag, 0.0)
    stacked = jnp.concatenate(
        [jnp.where(is_last[None], 0.0, forcing), left_spike[None], right_spike[None]], 0
    )
    solved = cyclic_reduce(low_inner, main_inner, high_inner, stacked, axis_dim, False)
    head_row = lax.slice_in_dim(solved, 0, 1, axis=axis_dim + 1)
    tail_row = lax.slice_in_dim(solved, length - 2, length - 1, axis=axis_dim + 1)
    low_last = lax.slice_in_dim(sub_diag, length - 1, length, axis=axis_dim)
    main_last = lax.slice_in_dim(main_diag, length - 1, length, axis=axis_dim)
    high_last = lax.slice_in_dim(super_diag, length - 1, length, axis=axis_dim)
    force_last = lax.slice_in_dim(forcing, length - 1, length, axis=axis_dim + 1)
    own_value, prev_value = interface(
        head_row, tail_row, low_last, main_last, high_last, force_last
    )
    inner_values = solved[:3] - solved[3][None] * prev_value - solved[4][None] * own_value
    return jnp.where(is_last[None], own_value, inner_values)


def pick_values(solution, members, my_index, axis_dim):
    own_value = lax.dynamic_slice_in_dim(solution, my_index, 1, axis_dim)
    prev_value = lax.dynamic_slice_in_dim(solution, (my_index + members - 1) % members, 1, axis_dim)
    return (own_value, prev_value)


def interface_x(head_row, tail_row, low_last, main_last, high_last, force_last):
    members = lax.axis_size("gx")
    my_index = lax.axis_index("gx")
    next_head = shifted_2(head_row, "gx", -1)
    rows_here = reduced_rows(tail_row, next_head, low_last, main_last, high_last, force_last)
    gathered = lax.all_gather(rows_here, "gx", axis=2, tiled=True)
    solution = cyclic_reduce(gathered[0], gathered[1], gathered[2], gathered[3:], 1, True)
    return pick_values(solution, members, my_index, 2)


def interface_y(head_row, tail_row, low_last, main_last, high_last, force_last):
    members = lax.axis_size("gy")
    next_head = shifted_2(head_row, "gy", -1)
    rows_here = reduced_rows(tail_row, next_head, low_last, main_last, high_last, force_last)
    gathered = lax.all_gather(rows_here, "gy", axis=3, tiled=True)
    solution = cyclic_reduce(gathered[0], gathered[1], gathered[2], gathered[3:], 2, True)
    return pick_values(solution, members, lax.axis_index("gy"), 3)


def lookup_phase(components, label_block):
    cell_tensor = jnp.zeros((5,) + label_block.shape, jnp.float32)
    for phase_id in range(components.shape[1]):
        cell_tensor = jnp.where(
            (label_block == phase_id)[None],
            components[:, phase_id][:, None, None, None],
            cell_tensor,
        )
    return cell_tensor


def local(potential, labels, principal, off_diagonal):
    components = jnp.concatenate([principal, off_diagonal], 0)
    cell_tensor = lookup_phase(components, labels)
    padded = padded_2(cell_tensor, (("gx", 2), ("gy", 3)), 1)
    damping = 2.0 / (potential.shape[3] * potential.shape[3])
    along_xdir = padded[:, :, :, 1:-1]
    cond_xx = along_xdir[0]
    face_east = harmonic(cond_xx[:, 1:-1], cond_xx[:, 2:])
    face_west = harmonic(cond_xx[:, :-2], cond_xx[:, 1:-1])
    source_x = jnp.stack(
        [
            face_east - face_west,
            0.5 * (along_xdir[2][:, 2:] - along_xdir[2][:, :-2]),
            0.5 * (along_xdir[3][:, 2:] - along_xdir[3][:, :-2]),
        ]
    )
    half_step = spike_solve(
        -face_west,
        damping + face_west + face_east,
        -face_east,
        damping * potential + source_x,
        1,
        interface_x,
    )
    along_ydir = padded[:, :, 1:-1, :]
    cond_yy = along_ydir[1]
    face_north = harmonic(cond_yy[:, :, 1:-1], cond_yy[:, :, 2:])
    face_south = harmonic(cond_yy[:, :, :-2], cond_yy[:, :, 1:-1])
    source_y = jnp.stack(
        [
            0.5 * (along_ydir[2][:, :, 2:] - along_ydir[2][:, :, :-2]),
            face_north - face_south,
            0.5 * (along_ydir[4][:, :, 2:] - along_ydir[4][:, :, :-2]),
        ]
    )
    return spike_solve(
        -face_south,
        damping + face_south + face_north,
        -face_north,
        damping * half_step + source_y,
        2,
        interface_y,
    )


def solution(mesh):
    in_specs = (P(None, None, "gx", "gy"), P(None, "gx", "gy"), P(), P())
    out_specs = P(None, None, "gx", "gy")
    return jax.shard_map(local, mesh=mesh, in_specs=in_specs, out_specs=out_specs, check_vma=False)
```

profile of v0, /device:TPU:0, one launch (start us, length us, event | category | flops | bytes accessed | tf_op | source)
XLA Modules:
  0.0 70.5 jit_solution(12789829236502406646)
XLA Ops:
  0.0 0.7 pad_maximum_fusion.15
  0.7 0.3 slice_reduce_fusion.9
  1.0 1.1 %compare_bitcast_fusion.7 = (pred[256,128]{1,0:T(8,128)(4,1)S(1)}, pred[256,128]{1,0:T(8,128)(4,1)S(1)}, pred[256,128]{1,0:T(8,128)(4,1)S(1)}, pred[256,128]{1,0...) fusion(s32[1,256,128]{2,1,0:T(8,128)} %param.5), kind=kLoop, calls=%fused_computation.147 | loop fusion | flops 262144 | bytes 393216 | tf_op jit(solution)/shard_map/jit(_where)/broadcast_in_dim | solution.py:136
  3.1 0.3 select_select_fusion
  3.6 5.5 %collective-permute-start.1 = (f32[5,1,1,128]{2,3,1,0:T(8,128)S(1)}, f32[5,1,1,128]{2,3,1,0:T(8,128)S(1)}, u32[]{:S(2)}, u32[]{:S(2)}) collective-permute-start(f32[5,1,1,128]{2,3,1,0:T(8,128)S(1)} %get-tuple-element.150), channel_id=1, source_target_pairs={{2,0},{4,2},{6,4},{8,6},{10,8},{12,10},{14,12},{16,14},{18,16},{20... | collective-permute-start | bytes 7688 | tf_op jit(solution)/shard_map/ppermute | solution.py:21
  9.0 0.6 iota_compare_fusion.5
  9.6 0.6 fusion.77
  10.2 0.5 iota_compare_fusion.4
  10.7 0.5 iota_compare_fusion.3
  11.2 0.6 fusion.76
  12.1 1.6 %collective-permute-done.1 = f32[5,1,1,128]{2,3,1,0:T(8,128)S(1)} collective-permute-done((f32[5,1,1,128]{2,3,1,0:T(8,128)S(1)}, f32[5,1,1,128]{2,3,1,0:T(8,128)S(1)}, u32[]{:S(2)}, u32[]{:S(2)}) %collective-permute-start.1) | collective-permute-done | bytes 2592 | tf_op jit(solution)/shard_map/ppermute | solution.py:21
  13.6 4.6 %collective-permute-done = f32[5,1,1,128]{2,3,1,0:T(8,128)S(1)} collective-permute-done((f32[5,1,1,128]{2,3,1,0:T(8,128)S(1)}, f32[5,1,1,128]{2,3,1,0:T(8,128)S(1)}, u32[]{:S(2)}, u32[]{:S(2)}) %collective-permute-start) | collective-permute-done | bytes 2592 | tf_op jit(solution)/shard_map/ppermute | solution.py:19
  18.2 0.3 maximum_bitcast_fusion
  18.7 0.7 broadcast_select_fusion.3
  19.9 0.2 fusion.131
  20.1 0.3 multiply_add_fusion.12
  20.4 0.2 fusion.130
  21.4 0.3 multiply_add_fusion.11
  21.6 0.2 fusion.129
  22.4 0.2 fusion.92
  22.6 0.3 multiply_add_fusion.10
  22.9 0.2 fusion.128
  23.8 0.3 multiply_add_fusion.9
  24.1 0.2 fusion.127
  24.8 0.2 fusion.96
  25.0 0.3 multiply_add_fusion.8
  25.3 0.2 fusion.126
  26.2 0.3 multiply_add_fusion.7
  26.5 0.2 fusion.125
  27.4 0.3 multiply_add_fusion.6
  28.8 0.7 %pad_maximum_fusion.13 = (f32[5,1,258,1]{2,3,1,0:T(1,128)}, f32[5,1,258,1]{2,3,1,0:T(1,128)}) fusion(f32[5,1,1,128]{2,3,1,0:T(8,128)S(1)} %collective-permute-done.1, f32[5,1,256,128]{2,3,1,0:T(8,128)S(1)} %select_select_fusion, f32[5,1,1,128]{2,3,1,0:T(8,128)S(1)} %collective-permute-done), kind=kLoop, calls=%fused_computation.248 | loop fusion | flops 5160 | bytes 670800 | tf_op jit(solution)/shard_map/slice | solution.py:16
  29.6 1.6 %collective-permute-start.3 = (f32[5,1,258,1]{2,3,1,0:T(1,128)}, f32[5,1,258,1]{2,3,1,0:T(1,128)S(1)}, u32[]{:S(2)}, u32[]{:S(2)}) collective-permute-start(f32[5,1,258,1]{2,3,1,0:T(1,128)} %get-tuple-element.112), channel_id=1, source_target_pairs={{1,0},{0,1},{3,2},{2,3},{5,4},{4,5},{7,6},{6,7},{9,8},{8,9},{11,10... | collective-permute-start | bytes 15488 | tf_op jit(solution)/shard_map/ppermute | solution.py:21
  31.2 0.5 collective-permute-start.2
  31.8 0.6 copy.142
  32.5 0.8 %collective-permute-done.4 = f32[5,1,1,128]{2,3,1,0:T(8,128)S(1)} collective-permute-done((f32[5,1,1,128]{2,3,1,0:T(8,128)S(1)}, f32[5,1,1,128]{2,3,1,0:T(8,128)S(1)}, u32[]{:S(2)}, u32[]{:S(2)}) %collective-permute-start.4) | collective-permute-done | bytes 2592 | tf_op jit(solution)/shard_map/ppermute | solution.py:9
  33.5 0.8 %copy-done.1 = f32[1,256,128]{1,2,0:T(8,128)S(1)} copy-done((f32[1,256,128]{1,2,0:T(8,128)S(1)}, f32[1,256,128]{1,2,0:T(8,128)}, u32[]{:S(2)}) %copy-start.1) | copy-done | bytes 131096
  34.3 0.3 fusion.24
  34.6 0.6 copy-done.2
  35.2 18.7 %all_gather.6 = f32[6,1,16,128]{3,1,0,2:T(1,128)S(1)} all-gather(f32[6,1,1,128]{3,1,0,2:T(1,128)S(1)} %maximum_bitcast_fusion.5), channel_id=1, replica_groups=mesh['gx'=16,'gy'=2] {'gx'}, dimensions={2}, use_global_device_ids=true | all-gather | bytes 52224 | tf_op jit(solution)/shard_map/all_gather | solution.py:119
  55.2 0.7 copy-done.3
  56.0 0.6 copy-done.9
  56.8 0.7 copy-done.5
  57.5 0.2 broadcast_select_fusion
  59.5 0.2 multiply_add_fusion.2
  61.2 1.6 %collective-permute-start.5 = (f32[5,1,256,1]{2,3,1,0:T(1,128)S(1)}, f32[5,1,256,1]{2,3,1,0:T(1,128)S(1)}, u32[]{:S(2)}, u32[]{:S(2)}) collective-permute-start(f32[5,1,256,1]{2,3,1,0:T(1,128)S(1)} %slice.1303), channel_id=1, source_target_pairs={{0,1},{1,0},{2,3},{3,2},{4,5},{5,4},{6,7},{7,6},{8,9},{9,8},{10,11... | collective-permute-start | bytes 15368 | tf_op jit(solution)/shard_map/ppermute | solution.py:9
  62.8 2.1 %collective-permute-done.5 = f32[5,1,256,1]{2,3,1,0:T(1,128)S(1)} collective-permute-done((f32[5,1,256,1]{2,3,1,0:T(1,128)S(1)}, f32[5,1,256,1]{2,3,1,0:T(1,128)S(1)}, u32[]{:S(2)}, u32[]{:S(2)}) %collective-permute-start.5) | collective-permute-done | bytes 5152 | tf_op jit(solution)/shard_map/ppermute | solution.py:9
  65.0 4.4 %all_gather.7 = f32[6,1,256,2]{2,1,0,3:T(1,128)S(1)} all-gather(f32[6,1,256,1]{2,1,0,3:T(1,128)S(1)} %maximum_bitcast_fusion.4), channel_id=1, replica_groups=mesh['gx'=16,'gy'=2] {'gy'}, dimensions={3}, use_global_device_ids=true | all-gather | bytes 18432 | tf_op jit(solution)/shard_map/all_gather | solution.py:128
  69.6 0.9 %copy.153 = f32[3,1,256,128]{3,2,1,0:T(8,128)} copy(f32[3,1,256,128]{2,3,1,0:T(8,128)S(1)} %fusion.1) | data formatting | bytes 786432 | tf_op jit(solution)/shard_map/jit(_where)/select_n | solution.py:105
  (213 shorter events, 11.4 us)
Async XLA Ops:
  3.4 8.5 %copy-start = (f32[3,1,256,128]{3,2,1,0:T(8,128)S(1)}, f32[3,1,256,128]{3,2,1,0:T(8,128)}, u32[]{:S(2)}) copy-start(f32[3,1,256,128]{3,2,1,0:T(8,128)} %param.4) | copy-start | bytes 1179652
  3.6 10.1 %collective-permute-start.1 = (f32[5,1,1,128]{2,3,1,0:T(8,128)S(1)}, f32[5,1,1,128]{2,3,1,0:T(8,128)S(1)}, u32[]{:S(2)}, u32[]{:S(2)}) collective-permute-start(f32[5,1,1,128]{2,3,1,0:T(8,128)S(1)} %get-tuple-element.150), channel_id=1, source_target_pairs={{2,0},{4,2},{6,4},{8,6},{10,8},{12,10},{14,12},{16,14},{18,16},{20... | collective-permute-start | bytes 7688 | tf_op jit(solution)/shard_map/ppermute | solution.py:21
  9.0 9.2 %collective-permute-start = (f32[5,1,1,128]{2,3,1,0:T(8,128)S(1)}, f32[5,1,1,128]{2,3,1,0:T(8,128)S(1)}, u32[]{:S(2)}, u32[]{:S(2)}) collective-permute-start(f32[5,1,1,128]{2,3,1,0:T(8,128)S(1)} %get-tuple-element.149), channel_id=1, source_target_pairs={{0,2},{2,4},{4,6},{6,8},{8,10},{10,12},{12,14},{14,16},{16,18},{18... | collective-permute-start | bytes 7688 | tf_op jit(solution)/shard_map/ppermute | solution.py:19
  11.8 7.9 %copy-start.4 = (pred[256]{0:T(512)(128)(4,1)}, pred[256]{0:T(512)(128)(4,1)S(1)}, u32[]{:S(2)}) copy-start(pred[256]{0:T(512)(128)(4,1)S(1)} %iota_compare_fusion.2) | copy-start | bytes 772
  28.6 4.8 %collective-permute-start.4 = (f32[5,1,1,128]{2,3,1,0:T(8,128)S(1)}, f32[5,1,1,128]{2,3,1,0:T(8,128)S(1)}, u32[]{:S(2)}, u32[]{:S(2)}) collective-permute-start(f32[5,1,1,128]{2,3,1,0:T(8,128)S(1)} %slice.1169), channel_id=1, source_target_pairs={{0,30},{2,0},{4,2},{6,4},{8,6},{10,8},{12,10},{14,12},{16,14},{18,... | collective-permute-start | bytes 7688 | tf_op jit(solution)/shard_map/ppermute | solution.py:9
  29.6 25.3 %collective-permute-start.3 = (f32[5,1,258,1]{2,3,1,0:T(1,128)}, f32[5,1,258,1]{2,3,1,0:T(1,128)S(1)}, u32[]{:S(2)}, u32[]{:S(2)}) collective-permute-start(f32[5,1,258,1]{2,3,1,0:T(1,128)} %get-tuple-element.112), channel_id=1, source_target_pairs={{1,0},{0,1},{3,2},{2,3},{5,4},{4,5},{7,6},{6,7},{9,8},{8,9},{11,10... | collective-permute-start | bytes 15488 | tf_op jit(solution)/shard_map/ppermute | solution.py:21
  31.2 23.7 %collective-permute-start.2 = (f32[5,1,258,1]{2,3,1,0:T(1,128)}, f32[5,1,258,1]{2,3,1,0:T(1,128)S(1)}, u32[]{:S(2)}, u32[]{:S(2)}) collective-permute-start(f32[5,1,258,1]{2,3,1,0:T(1,128)} %get-tuple-element.111), channel_id=1, source_target_pairs={{0,1},{1,0},{2,3},{3,2},{4,5},{5,4},{6,7},{7,6},{8,9},{9,8},{10,11... | collective-permute-start | bytes 15488 | tf_op jit(solution)/shard_map/ppermute | solution.py:19
  33.4 0.9 %copy-start.1 = (f32[1,256,128]{1,2,0:T(8,128)S(1)}, f32[1,256,128]{1,2,0:T(8,128)}, u32[]{:S(2)}) copy-start(f32[1,256,128]{1,2,0:T(8,128)} %get-tuple-element.102) | copy-start | bytes 393220
  34.6 0.6 copy-start.2
  55.2 0.7 copy-start.3
  55.9 0.7 copy-start.9
  56.0 0.7 copy-start.6
  56.0 0.7 copy-start.7
  56.0 0.6 copy-start.8
  56.8 0.7 copy-start.5
  61.2 3.7 %collective-permute-start.5 = (f32[5,1,256,1]{2,3,1,0:T(1,128)S(1)}, f32[5,1,256,1]{2,3,1,0:T(1,128)S(1)}, u32[]{:S(2)}, u32[]{:S(2)}) collective-permute-start(f32[5,1,256,1]{2,3,1,0:T(1,128)S(1)} %slice.1303), channel_id=1, source_target_pairs={{0,1},{1,0},{2,3},{3,2},{4,5},{5,4},{6,7},{7,6},{8,9},{9,8},{10,11... | collective-permute-start | bytes 15368 | tf_op jit(solution)/shard_map/ppermute | solution.py:9
where the time goes:
time: 70.8 us; the launch traced here: 70.5 us
  blocking collectives  23.1 us (33%)
  other arithmetic  15.5 us (22%)
  local copies, waits for them, and re-layouts  12 us (17%)
  starting transfers between devices  9.31 us (13%)
  waiting for transfers between devices  9.1 us (13%)
  between operations  1.55 us (2%)
    all_gather x1, blocking collectives, interface_x(): gathered = lax.all_gather(rows_here, 'gx', axis=2, tiled=True)  18.7 us
    ppermute x2, starting transfers between devices, padded_2(): lax.ppermute(head, axis, [((i + 1) % count, i) for i in range(count)])  7.05 us
    ppermute x2, waiting for transfers between devices, padded_2(): lax.ppermute(tail, axis, [(i, (i + 1) % count) for i in range(count)])  4.61 us
    all_gather x1, blocking collectives, interface_y(): gathered = lax.all_gather(rows_here, 'gy', axis=3, tiled=True)  4.36 us
    slice x47, local copies, waits for them, and re-layouts, neighbour(): retained = lax.slice_in_dim(values, 0, extent - offset, axis=axis_dim)  3.91 us
    unnamed x28, local copies, waits for them, and re-layouts  3.57 us
    add x16, other arithmetic, cyclic_reduce(): forcing + factor_low[None] * rest_before + factor_high[None] * rest_after  3.03 us
    ppermute x2, waiting for transfers between devices, shifted_2(): lax.ppermute(shard, axis, [(i, (i + by) % size) for i in range(size)])  2.92 us
  transfers between devices with their start and end apart: 6, of which 4 were waited for; matrix products, arithmetic and copies ran while one was open for 8% of the time, Pallas kernels for 0%

commit v1 on v0

--- a/solution.py
+++ b/solution.py
@@ -116,7 +116,12 @@
     my_index = lax.axis_index("gx")
     next_head = shifted_2(head_row, "gx", -1)
     rows_here = reduced_rows(tail_row, next_head, low_last, main_last, high_last, force_last)
-    gathered = lax.all_gather(rows_here, "gx", axis=2, tiled=True)
+    ring = [rows_here]
+    for hop in range(15):
+        ring.append(lax.ppermute(ring[-1], "gx", [(dev, (dev + 1) % 16) for dev in range(16)]))
+    gathered = jnp.roll(
+        jnp.concatenate(ring[::-1], axis=2), (lax.axis_index("gx") + 1) * ring[0].shape[2], axis=2
+    )
     solution = cyclic_reduce(gathered[0], gathered[1], gathered[2], gathered[3:], 1, True)
     return pick_values(solution, members, my_index, 2)
 

time: 70.8 us -> 142 us (2.01)
  waiting for transfers between devices: 9.1 us -> 84.2 us
  blocking collectives: 23.1 us -> 4.36 us
  local copies, waits for them, and re-layouts: 12 us -> 23.9 us
  other arithmetic: 15.5 us -> 17.8 us
    ppermute x0 -> x15, waiting for transfers between devices: none -> 74 us  [interface_x(): lax.ppermute(ring[-1], 'gx', [(dev, (dev + 1) % 16) for dev in range(16)])]
    all_gather x1 -> x0, blocking collectives: 18.7 us -> none  [interface_x(): gathered = lax.all_gather(rows_here, 'gx', axis=2, tiled=True)]
    unnamed x28 -> x52, local copies, waits for them, and re-layouts: 3.57 us -> 9.86 us
    concatenate x0 -> x1, local copies, waits for them, and re-layouts: none -> 5.39 us  [interface_x(): jnp.roll(jnp.concatenate(ring[::-1], axis=2), (lax.axis_index('gx') + 1)...]
  transfers between devices with their start and end apart: 6 -> 21, of which waited for: 4 -> 20; matrix products, arithmetic and copies ran while one was open for 8% -> 6% of each run, Pallas kernels for 0% -> 0%
where the time goes in v1:
time: 142 us; the launch traced here: 141 us
  waiting for transfers between devices  84.2 us (59%)
  local copies, waits for them, and re-layouts  23.9 us (17%)
  other arithmetic  17.8 us (13%)
  starting transfers between devices  9.41 us (7%)
  blocking collectives  4.36 us (3%)
  between operations  1.55 us (1%)
    ppermute x15, waiting for transfers between devices, interface_x(): lax.ppermute(ring[-1], 'gx', [(dev, (dev + 1) % 16) for dev in range(16)])  74 us
    unnamed x52, local copies, waits for them, and re-layouts  9.86 us
    ppermute x2, starting transfers between devices, padded_2(): lax.ppermute(head, axis, [((i + 1) % count, i) for i in range(count)])  7.05 us
    concatenate x1, local copies, waits for them, and re-layouts, interface_x(): jnp.roll(jnp.concatenate(ring[::-1], axis=2), (lax.axis_index('gx') + 1)...  5.39 us
    ppermute x2, waiting for transfers between devices, padded_2(): lax.ppermute(tail, axis, [(i, (i + 1) % count) for i in range(count)])  5.05 us
    all_gather x1, blocking collectives, interface_y(): gathered = lax.all_gather(rows_here, 'gy', axis=3, tiled=True)  4.36 us
    slice x47, local copies, waits for them, and re-layouts, neighbour(): retained = lax.slice_in_dim(values, 0, extent - offset, axis=axis_dim)  3.94 us
    ppermute x2, waiting for transfers between devices, shifted_2(): lax.ppermute(shard, axis, [(i, (i + by) % size) for i in range(size)])  3.43 us
  transfers between devices with their start and end apart: 21, of which 20 were waited for; matrix products, arithmetic and copies ran while one was open for 6% of the time, Pallas kernels for 0%

profile of v1, /device:TPU:0, one launch (start us, length us, event | category | flops | bytes accessed | tf_op | source)
XLA Modules:
  0.0 141.2 jit_solution(3635747334085594509)
XLA Ops:
  0.0 0.7 pad_maximum_fusion.15
  1.0 1.1 compare_bitcast_fusion.7
  3.6 5.5 %collective-permute-start.1 = (f32[5,1,1,128]{2,3,1,0:T(8,128)S(1)}, f32[5,1,1,128]{2,3,1,0:T(8,128)S(1)}, u32[]{:S(2)}, u32[]{:S(2)}) collective-permute-start(f32[5,1,1,128]{2,3,1,0:T(8,128)S(1)} %get-tuple-element.150), channel_id=1, source_target_pairs={{2,0},{4,2},{6,4},{8,6},{10,8},{12,10},{14,12},{16,14},{18,16},{20... | collective-permute-start | bytes 7688 | tf_op jit(solution)/shard_map/ppermute | solution.py:21
  9.0 0.6 iota_compare_fusion.5
  9.6 0.5 fusion.77
  12.0 1.7 %collective-permute-done.1 = f32[5,1,1,128]{2,3,1,0:T(8,128)S(1)} collective-permute-done((f32[5,1,1,128]{2,3,1,0:T(8,128)S(1)}, f32[5,1,1,128]{2,3,1,0:T(8,128)S(1)}, u32[]{:S(2)}, u32[]{:S(2)}) %collective-permute-start.1) | collective-permute-done | bytes 2592 | tf_op jit(solution)/shard_map/ppermute | solution.py:21
  13.6 4.6 %collective-permute-done = f32[5,1,1,128]{2,3,1,0:T(8,128)S(1)} collective-permute-done((f32[5,1,1,128]{2,3,1,0:T(8,128)S(1)}, f32[5,1,1,128]{2,3,1,0:T(8,128)S(1)}, u32[]{:S(2)}, u32[]{:S(2)}) %collective-permute-start) | collective-permute-done | bytes 2592 | tf_op jit(solution)/shard_map/ppermute | solution.py:19
  18.7 0.7 broadcast_select_fusion.3
  28.8 0.7 pad_maximum_fusion.13
  29.6 1.6 %collective-permute-start.3 = (f32[5,1,258,1]{2,3,1,0:T(1,128)}, f32[5,1,258,1]{2,3,1,0:T(1,128)S(1)}, u32[]{:S(2)}, u32[]{:S(2)}) collective-permute-start(f32[5,1,258,1]{2,3,1,0:T(1,128)} %get-tuple-element.112), channel_id=1, source_target_pairs={{1,0},{0,1},{3,2},{2,3},{5,4},{4,5},{7,6},{6,7},{9,8},{8,9},{11,10... | collective-permute-start | bytes 15488 | tf_op jit(solution)/shard_map/ppermute | solution.py:21
  32.0 1.4 collective-permute-done.4
  33.5 0.8 copy-done.2
  35.1 0.8 maximum_bitcast_fusion.2
  36.0 0.8 fusion.108
  36.7 0.7 copy-done.14
  37.4 0.7 broadcast_select_fusion.2
  38.1 0.6 copy-done.18
  40.6 5.7 %collective-permute-done.6 = f32[6,1,1,128]{3,2,1,0:T(1,128)S(1)} collective-permute-done((f32[6,1,1,128]{3,2,1,0:T(1,128)S(1)}, f32[6,1,1,128]{3,2,1,0:T(1,128)S(1)}, u32[]{:S(2)}, u32[]{:S(2)}) %collective-permute-start.6) | collective-permute-done | bytes 3104 | tf_op jit(solution)/shard_map/ppermute | solution.py:121
  46.3 5.7 %collective-permute-done.7 = f32[6,1,1,128]{3,2,1,0:T(1,128)S(1)} collective-permute-done((f32[6,1,1,128]{3,2,1,0:T(1,128)S(1)}, f32[6,1,1,128]{3,2,1,0:T(1,128)S(1)}, u32[]{:S(2)}, u32[]{:S(2)}) %collective-permute-start.7) | collective-permute-done | bytes 3104 | tf_op jit(solution)/shard_map/ppermute | solution.py:121
  52.1 5.7 %collective-permute-done.8 = f32[6,1,1,128]{3,2,1,0:T(1,128)S(1)} collective-permute-done((f32[6,1,1,128]{3,2,1,0:T(1,128)S(1)}, f32[6,1,1,128]{3,2,1,0:T(1,128)S(1)}, u32[]{:S(2)}, u32[]{:S(2)}) %collective-permute-start.8) | collective-permute-done | bytes 3104 | tf_op jit(solution)/shard_map/ppermute | solution.py:121
  57.7 0.6 copy-done.3
  58.3 5.1 %collective-permute-done.9 = f32[6,1,1,128]{3,2,1,0:T(1,128)S(1)} collective-permute-done((f32[6,1,1,128]{3,2,1,0:T(1,128)S(1)}, f32[6,1,1,128]{3,2,1,0:T(1,128)S(1)}, u32[]{:S(2)}, u32[]{:S(2)}) %collective-permute-start.9) | collective-permute-done | bytes 3104 | tf_op jit(solution)/shard_map/ppermute | solution.py:121
  63.5 0.5 copy-done.4
  64.0 5.1 %collective-permute-done.10 = f32[6,1,1,128]{3,2,1,0:T(1,128)S(1)} collective-permute-done((f32[6,1,1,128]{3,2,1,0:T(1,128)S(1)}, f32[6,1,1,128]{3,2,1,0:T(1,128)S(1)}, u32[]{:S(2)}, u32[]{:S(2)}) %collective-permute-start.10) | collective-permute-done | bytes 3104 | tf_op jit(solution)/shard_map/ppermute | solution.py:121
  69.2 0.6 copy-done.5
  69.8 5.1 %collective-permute-done.11 = f32[6,1,1,128]{3,2,1,0:T(1,128)S(1)} collective-permute-done((f32[6,1,1,128]{3,2,1,0:T(1,128)S(1)}, f32[6,1,1,128]{3,2,1,0:T(1,128)S(1)}, u32[]{:S(2)}, u32[]{:S(2)}) %collective-permute-start.11) | collective-permute-done | bytes 3104 | tf_op jit(solution)/shard_map/ppermute | solution.py:121
  75.5 5.1 %collective-permute-done.12 = f32[6,1,1,128]{3,2,1,0:T(1,128)S(1)} collective-permute-done((f32[6,1,1,128]{3,2,1,0:T(1,128)S(1)}, f32[6,1,1,128]{3,2,1,0:T(1,128)S(1)}, u32[]{:S(2)}, u32[]{:S(2)}) %collective-permute-start.12) | collective-permute-done | bytes 3104 | tf_op jit(solution)/shard_map/ppermute | solution.py:121
  80.6 0.6 copy-done.7
  81.2 5.1 %collective-permute-done.13 = f32[6,1,1,128]{3,2,1,0:T(1,128)S(1)} collective-permute-done((f32[6,1,1,128]{3,2,1,0:T(1,128)S(1)}, f32[6,1,1,128]{3,2,1,0:T(1,128)S(1)}, u32[]{:S(2)}, u32[]{:S(2)}) %collective-permute-start.13) | collective-permute-done | bytes 3104 | tf_op jit(solution)/shard_map/ppermute | solution.py:121
  86.9 5.1 %collective-permute-done.14 = f32[6,1,1,128]{3,2,1,0:T(1,128)S(1)} collective-permute-done((f32[6,1,1,128]{3,2,1,0:T(1,128)S(1)}, f32[6,1,1,128]{3,2,1,0:T(1,128)S(1)}, u32[]{:S(2)}, u32[]{:S(2)}) %collective-permute-start.14) | collective-permute-done | bytes 3104 | tf_op jit(solution)/shard_map/ppermute | solution.py:121
  92.1 0.5 copy-done.9
  92.6 5.1 %collective-permute-done.15 = f32[6,1,1,128]{3,2,1,0:T(1,128)S(1)} collective-permute-done((f32[6,1,1,128]{3,2,1,0:T(1,128)S(1)}, f32[6,1,1,128]{3,2,1,0:T(1,128)S(1)}, u32[]{:S(2)}, u32[]{:S(2)}) %collective-permute-start.15) | collective-permute-done | bytes 3104 | tf_op jit(solution)/shard_map/ppermute | solution.py:121
  97.8 0.6 copy-done.10
  98.4 5.1 %collective-permute-done.16 = f32[6,1,1,128]{3,2,1,0:T(1,128)S(1)} collective-permute-done((f32[6,1,1,128]{3,2,1,0:T(1,128)S(1)}, f32[6,1,1,128]{3,2,1,0:T(1,128)S(1)}, u32[]{:S(2)}, u32[]{:S(2)}) %collective-permute-start.16) | collective-permute-done | bytes 3104 | tf_op jit(solution)/shard_map/ppermute | solution.py:121
  103.5 0.6 copy-done.11
  104.1 5.1 %collective-permute-done.17 = f32[6,1,1,128]{3,2,1,0:T(1,128)S(1)} collective-permute-done((f32[6,1,1,128]{3,2,1,0:T(1,128)S(1)}, f32[6,1,1,128]{3,2,1,0:T(1,128)S(1)}, u32[]{:S(2)}, u32[]{:S(2)}) %collective-permute-start.17) | collective-permute-done | bytes 3104 | tf_op jit(solution)/shard_map/ppermute | solution.py:121
  109.2 0.6 copy-done.12
  109.8 5.1 %collective-permute-done.18 = f32[6,1,1,128]{3,2,1,0:T(1,128)S(1)} collective-permute-done((f32[6,1,1,128]{3,2,1,0:T(1,128)S(1)}, f32[6,1,1,128]{3,2,1,0:T(1,128)S(1)}, u32[]{:S(2)}, u32[]{:S(2)}) %collective-permute-start.18) | collective-permute-done | bytes 3104 | tf_op jit(solution)/shard_map/ppermute | solution.py:121
  115.5 5.2 %collective-permute-done.19 = f32[6,1,1,128]{3,2,1,0:T(1,128)} collective-permute-done((f32[6,1,1,128]{3,2,1,0:T(1,128)S(1)}, f32[6,1,1,128]{3,2,1,0:T(1,128)}, u32[]{:S(2)}, u32[]{:S(2)}) %collective-permute-start.19) | collective-permute-done | bytes 3104 | tf_op jit(solution)/shard_map/ppermute | solution.py:121
  120.8 5.4 %concatenate.1220 = f32[6,1,32,128]{3,2,1,0:T(8,128)} concatenate(f32[6,1,1,128]{3,2,1,0:T(1,128)} %collective-permute-done.19, f32[6,1,1,128]{3,2,1,0:T(1,128)} %copy-done.13, f32[6,1,1,128]{3,2,1,0:T(1,128)} %copy-done.12, f32[6,1,1,128]{3,2,1,0:T(1,128)} %copy-done.11, f32[6,1,1,128]{3,2,1,0:T(1,128)} %copy-done.10, f32[6,1,1,128]{3,2,1,0:T(1,128)} %copy-done.9, ...), dimensions={2} | concatenate | bytes 196608 | tf_op jit(solution)/shard_map/jit(_roll_dynamic)/concatenate | solution.py:122
  126.1 0.7 dynamic-slice_bitcast_fusion
  127.2 0.8 copy-done
  128.5 0.7 copy-done.15
  131.2 1.6 %collective-permute-start.20 = (f32[5,1,256,1]{2,3,1,0:T(1,128)S(1)}, f32[5,1,256,1]{2,3,1,0:T(1,128)S(1)}, u32[]{:S(2)}, u32[]{:S(2)}) collective-permute-start(f32[5,1,256,1]{2,3,1,0:T(1,128)S(1)} %slice.1295), channel_id=1, source_target_pairs={{0,1},{1,0},{2,3},{3,2},{4,5},{5,4},{6,7},{7,6},{8,9},{9,8},{10,11... | collective-permute-start | bytes 15368 | tf_op jit(solution)/shard_map/ppermute | solution.py:9
  132.8 2.1 %collective-permute-done.20 = f32[5,1,256,1]{2,3,1,0:T(1,128)S(1)} collective-permute-done((f32[5,1,256,1]{2,3,1,0:T(1,128)S(1)}, f32[5,1,256,1]{2,3,1,0:T(1,128)S(1)}, u32[]{:S(2)}, u32[]{:S(2)}) %collective-permute-start.20) | collective-permute-done | bytes 5152 | tf_op jit(solution)/shard_map/ppermute | solution.py:9
  134.9 0.7 fusion.74
  135.6 4.4 %all_gather.3 = f32[6,1,256,2]{2,1,0,3:T(1,128)S(1)} all-gather(f32[6,1,256,1]{2,1,0,3:T(1,128)S(1)} %maximum_bitcast_fusion.4), channel_id=1, replica_groups=mesh['gx'=16,'gy'=2] {'gy'}, dimensions={3}, use_global_device_ids=true | all-gather | bytes 18432 | tf_op jit(solution)/shard_map/all_gather | solution.py:133
  140.3 0.9 copy.141
  (267 shorter events, 21.0 us)
Async XLA Ops:
  3.4 8.3 %copy-start.1 = (f32[3,1,256,128]{3,2,1,0:T(8,128)S(1)}, f32[3,1,256,128]{3,2,1,0:T(8,128)}, u32[]{:S(2)}) copy-start(f32[3,1,256,128]{3,2,1,0:T(8,128)} %param.4) | copy-start | bytes 1179652
  3.6 10.1 %collective-permute-start.1 = (f32[5,1,1,128]{2,3,1,0:T(8,128)S(1)}, f32[5,1,1,128]{2,3,1,0:T(8,128)S(1)}, u32[]{:S(2)}, u32[]{:S(2)}) collective-permute-start(f32[5,1,1,128]{2,3,1,0:T(8,128)S(1)} %get-tuple-element.150), channel_id=1, source_target_pairs={{2,0},{4,2},{6,4},{8,6},{10,8},{12,10},{14,12},{16,14},{18,16},{20... | collective-permute-start | bytes 7688 | tf_op jit(solution)/shard_map/ppermute | solution.py:21
  9.0 9.2 %collective-permute-start = (f32[5,1,1,128]{2,3,1,0:T(8,128)S(1)}, f32[5,1,1,128]{2,3,1,0:T(8,128)S(1)}, u32[]{:S(2)}, u32[]{:S(2)}) collective-permute-start(f32[5,1,1,128]{2,3,1,0:T(8,128)S(1)} %get-tuple-element.149), channel_id=1, source_target_pairs={{0,2},{2,4},{4,6},{6,8},{8,10},{10,12},{12,14},{14,16},{16,18},{18... | collective-permute-start | bytes 7688 | tf_op jit(solution)/shard_map/ppermute | solution.py:19
  11.7 8.1 %copy-start.16 = (pred[256]{0:T(512)(128)(4,1)}, pred[256]{0:T(512)(128)(4,1)S(1)}, u32[]{:S(2)}) copy-start(pred[256]{0:T(512)(128)(4,1)S(1)} %iota_compare_fusion.2) | copy-start | bytes 772
  28.6 4.8 %collective-permute-start.4 = (f32[5,1,1,128]{2,3,1,0:T(8,128)S(1)}, f32[5,1,1,128]{2,3,1,0:T(8,128)S(1)}, u32[]{:S(2)}, u32[]{:S(2)}) collective-permute-start(f32[5,1,1,128]{2,3,1,0:T(8,128)S(1)} %slice.1169), channel_id=1, source_target_pairs={{0,30},{2,0},{4,2},{6,4},{8,6},{10,8},{12,10},{14,12},{16,14},{18,... | collective-permute-start | bytes 7688 | tf_op jit(solution)/shard_map/ppermute | solution.py:9
  29.6 5.1 %collective-permute-start.3 = (f32[5,1,258,1]{2,3,1,0:T(1,128)}, f32[5,1,258,1]{2,3,1,0:T(1,128)S(1)}, u32[]{:S(2)}, u32[]{:S(2)}) collective-permute-start(f32[5,1,258,1]{2,3,1,0:T(1,128)} %get-tuple-element.112), channel_id=1, source_target_pairs={{1,0},{0,1},{3,2},{2,3},{5,4},{4,5},{7,6},{6,7},{9,8},{8,9},{11,10... | collective-permute-start | bytes 15488 | tf_op jit(solution)/shard_map/ppermute | solution.py:21
  31.2 4.0 %collective-permute-start.2 = (f32[5,1,258,1]{2,3,1,0:T(1,128)}, f32[5,1,258,1]{2,3,1,0:T(1,128)}, u32[]{:S(2)}, u32[]{:S(2)}) collective-permute-start(f32[5,1,258,1]{2,3,1,0:T(1,128)} %get-tuple-element.111), channel_id=1, source_target_pairs={{0,1},{1,0},{2,3},{3,2},{4,5},{5,4},{6,7},{7,6},{8,9},{9,8},{10,11... | collective-permute-start | bytes 15488 | tf_op jit(solution)/shard_map/ppermute | solution.py:19
  33.4 0.9 copy-start.2
  34.6 5.9 %collective-permute-start.5 = (f32[6,1,1,128]{3,2,1,0:T(1,128)S(1)}, f32[6,1,1,128]{3,2,1,0:T(1,128)S(1)}, u32[]{:S(2)}, u32[]{:S(2)}) collective-permute-start(f32[6,1,1,128]{3,2,1,0:T(1,128)S(1)} %pad_maximum_fusion.16), channel_id=1, source_target_pairs={{0,2},{2,4},{4,6},{6,8},{8,10},{10,12},{12,14},{14,16},{16,18},{18... | collective-permute-start | bytes 9224 | tf_op jit(solution)/shard_map/ppermute | solution.py:121
  36.7 0.7 copy-start.14
  37.4 0.7 copy-start.21
  38.1 0.6 copy-start.18
  38.1 0.6 copy-start.19
  38.1 0.6 copy-start.20
  40.6 5.7 %collective-permute-start.6 = (f32[6,1,1,128]{3,2,1,0:T(1,128)S(1)}, f32[6,1,1,128]{3,2,1,0:T(1,128)S(1)}, u32[]{:S(2)}, u32[]{:S(2)}) collective-permute-start(f32[6,1,1,128]{3,2,1,0:T(1,128)S(1)} %collective-permute-done.5), channel_id=1, source_target_pairs={{0,2},{2,4},{4,6},{6,8},{8,10},{10,12},{12,14},{14,16},{16,18},{18... | collective-permute-start | bytes 9224 | tf_op jit(solution)/shard_map/ppermute | solution.py:121
  46.3 5.7 %collective-permute-start.7 = (f32[6,1,1,128]{3,2,1,0:T(1,128)S(1)}, f32[6,1,1,128]{3,2,1,0:T(1,128)S(1)}, u32[]{:S(2)}, u32[]{:S(2)}) collective-permute-start(f32[6,1,1,128]{3,2,1,0:T(1,128)S(1)} %collective-permute-done.6), channel_id=1, source_target_pairs={{0,2},{2,4},{4,6},{6,8},{8,10},{10,12},{12,14},{14,16},{16,18},{18... | collective-permute-start | bytes 9224 | tf_op jit(solution)/shard_map/ppermute | solution.py:121
  52.0 5.7 %collective-permute-start.8 = (f32[6,1,1,128]{3,2,1,0:T(1,128)S(1)}, f32[6,1,1,128]{3,2,1,0:T(1,128)S(1)}, u32[]{:S(2)}, u32[]{:S(2)}) collective-permute-start(f32[6,1,1,128]{3,2,1,0:T(1,128)S(1)} %collective-permute-done.7), channel_id=1, source_target_pairs={{0,2},{2,4},{4,6},{6,8},{8,10},{10,12},{12,14},{14,16},{16,18},{18... | collective-permute-start | bytes 9224 | tf_op jit(solution)/shard_map/ppermute | solution.py:121
  57.7 0.6 copy-start.3
  57.7 5.7 %collective-permute-start.9 = (f32[6,1,1,128]{3,2,1,0:T(1,128)S(1)}, f32[6,1,1,128]{3,2,1,0:T(1,128)S(1)}, u32[]{:S(2)}, u32[]{:S(2)}) collective-permute-start(f32[6,1,1,128]{3,2,1,0:T(1,128)S(1)} %collective-permute-done.8), channel_id=1, source_target_pairs={{0,2},{2,4},{4,6},{6,8},{8,10},{10,12},{12,14},{14,16},{16,18},{18... | collective-permute-start | bytes 9224 | tf_op jit(solution)/shard_map/ppermute | solution.py:121
  63.4 0.6 copy-start.4
  63.4 5.7 %collective-permute-start.10 = (f32[6,1,1,128]{3,2,1,0:T(1,128)S(1)}, f32[6,1,1,128]{3,2,1,0:T(1,128)S(1)}, u32[]{:S(2)}, u32[]{:S(2)}) collective-permute-start(f32[6,1,1,128]{3,2,1,0:T(1,128)S(1)} %collective-permute-done.9), channel_id=1, source_target_pairs={{0,2},{2,4},{4,6},{6,8},{8,10},{10,12},{12,14},{14,16},{16,18},{18... | collective-permute-start | bytes 9224 | tf_op jit(solution)/shard_map/ppermute | solution.py:121
  69.2 0.6 copy-start.5
  69.2 5.7 %collective-permute-start.11 = (f32[6,1,1,128]{3,2,1,0:T(1,128)S(1)}, f32[6,1,1,128]{3,2,1,0:T(1,128)S(1)}, u32[]{:S(2)}, u32[]{:S(2)}) collective-permute-start(f32[6,1,1,128]{3,2,1,0:T(1,128)S(1)} %collective-permute-done.10), channel_id=1, source_target_pairs={{0,2},{2,4},{4,6},{6,8},{8,10},{10,12},{12,14},{14,16},{16,18},{18... | collective-permute-start | bytes 9224 | tf_op jit(solution)/shard_map/ppermute | solution.py:121
  74.9 0.6 copy-start.6
  74.9 5.7 %collective-permute-start.12 = (f32[6,1,1,128]{3,2,1,0:T(1,128)S(1)}, f32[6,1,1,128]{3,2,1,0:T(1,128)S(1)}, u32[]{:S(2)}, u32[]{:S(2)}) collective-permute-start(f32[6,1,1,128]{3,2,1,0:T(1,128)S(1)} %collective-permute-done.11), channel_id=1, source_target_pairs={{0,2},{2,4},{4,6},{6,8},{8,10},{10,12},{12,14},{14,16},{16,18},{18... | collective-permute-start | bytes 9224 | tf_op jit(solution)/shard_map/ppermute | solution.py:121
  80.6 0.6 copy-start.7
  80.6 5.7 %collective-permute-start.13 = (f32[6,1,1,128]{3,2,1,0:T(1,128)S(1)}, f32[6,1,1,128]{3,2,1,0:T(1,128)S(1)}, u32[]{:S(2)}, u32[]{:S(2)}) collective-permute-start(f32[6,1,1,128]{3,2,1,0:T(1,128)S(1)} %collective-permute-done.12), channel_id=1, source_target_pairs={{0,2},{2,4},{4,6},{6,8},{8,10},{10,12},{12,14},{14,16},{16,18},{18... | collective-permute-start | bytes 9224 | tf_op jit(solution)/shard_map/ppermute | solution.py:121
  86.3 0.6 copy-start.8
  86.3 5.7 %collective-permute-start.14 = (f32[6,1,1,128]{3,2,1,0:T(1,128)S(1)}, f32[6,1,1,128]{3,2,1,0:T(1,128)S(1)}, u32[]{:S(2)}, u32[]{:S(2)}) collective-permute-start(f32[6,1,1,128]{3,2,1,0:T(1,128)S(1)} %collective-permute-done.13), channel_id=1, source_target_pairs={{0,2},{2,4},{4,6},{6,8},{8,10},{10,12},{12,14},{14,16},{16,18},{18... | collective-permute-start | bytes 9224 | tf_op jit(solution)/shard_map/ppermute | solution.py:121
  92.0 0.6 copy-start.9
  92.0 5.7 %collective-permute-start.15 = (f32[6,1,1,128]{3,2,1,0:T(1,128)S(1)}, f32[6,1,1,128]{3,2,1,0:T(1,128)S(1)}, u32[]{:S(2)}, u32[]{:S(2)}) collective-permute-start(f32[6,1,1,128]{3,2,1,0:T(1,128)S(1)} %collective-permute-done.14), channel_id=1, source_target_pairs={{0,2},{2,4},{4,6},{6,8},{8,10},{10,12},{12,14},{14,16},{16,18},{18... | collective-permute-start | bytes 9224 | tf_op jit(solution)/shard_map/ppermute | solution.py:121
  97.8 0.6 copy-start.10
  97.8 5.7 %collective-permute-start.16 = (f32[6,1,1,128]{3,2,1,0:T(1,128)S(1)}, f32[6,1,1,128]{3,2,1,0:T(1,128)S(1)}, u32[]{:S(2)}, u32[]{:S(2)}) collective-permute-start(f32[6,1,1,128]{3,2,1,0:T(1,128)S(1)} %collective-permute-done.15), channel_id=1, source_target_pairs={{0,2},{2,4},{4,6},{6,8},{8,10},{10,12},{12,14},{14,16},{16,18},{18... | collective-permute-start | bytes 9224 | tf_op jit(solution)/shard_map/ppermute | solution.py:121
  103.5 0.6 copy-start.11
  103.5 5.7 %collective-permute-start.17 = (f32[6,1,1,128]{3,2,1,0:T(1,128)S(1)}, f32[6,1,1,128]{3,2,1,0:T(1,128)S(1)}, u32[]{:S(2)}, u32[]{:S(2)}) collective-permute-start(f32[6,1,1,128]{3,2,1,0:T(1,128)S(1)} %collective-permute-done.16), channel_id=1, source_target_pairs={{0,2},{2,4},{4,6},{6,8},{8,10},{10,12},{12,14},{14,16},{16,18},{18... | collective-permute-start | bytes 9224 | tf_op jit(solution)/shard_map/ppermute | solution.py:121
  109.2 0.6 copy-start.12
  109.2 5.7 %collective-permute-start.18 = (f32[6,1,1,128]{3,2,1,0:T(1,128)S(1)}, f32[6,1,1,128]{3,2,1,0:T(1,128)S(1)}, u32[]{:S(2)}, u32[]{:S(2)}) collective-permute-start(f32[6,1,1,128]{3,2,1,0:T(1,128)S(1)} %collective-permute-done.17), channel_id=1, source_target_pairs={{0,2},{2,4},{4,6},{6,8},{8,10},{10,12},{12,14},{14,16},{16,18},{18... | collective-permute-start | bytes 9224 | tf_op jit(solution)/shard_map/ppermute | solution.py:121
  114.9 0.6 copy-start.13
  114.9 5.8 %collective-permute-start.19 = (f32[6,1,1,128]{3,2,1,0:T(1,128)S(1)}, f32[6,1,1,128]{3,2,1,0:T(1,128)}, u32[]{:S(2)}, u32[]{:S(2)}) collective-permute-start(f32[6,1,1,128]{3,2,1,0:T(1,128)S(1)} %collective-permute-done.18), channel_id=1, source_target_pairs={{0,2},{2,4},{4,6},{6,8},{8,10},{10,12},{12,14},{14,16},{16,18},{18... | collective-permute-start | bytes 9224 | tf_op jit(solution)/shard_map/ppermute | solution.py:121
  127.1 0.9 copy-start
  128.4 0.7 copy-start.15
  128.4 0.7 copy-start.17
  131.2 3.7 %collective-permute-start.20 = (f32[5,1,256,1]{2,3,1,0:T(1,128)S(1)}, f32[5,1,256,1]{2,3,1,0:T(1,128)S(1)}, u32[]{:S(2)}, u32[]{:S(2)}) collective-permute-start(f32[5,1,256,1]{2,3,1,0:T(1,128)S(1)} %slice.1295), channel_id=1, source_target_pairs={{0,1},{1,0},{2,3},{3,2},{4,5},{5,4},{6,7},{7,6},{8,9},{9,8},{10,11... | collective-permute-start | bytes 15368 | tf_op jit(solution)/shard_map/ppermute | solution.py:9
